TPU v7x, 256 devices: a whole 4x4x8 slice. The times are simulated.
256 devices in a mesh: bin: 4 (over x_lo, core), row: 64 (over z, x_hi, y).
Axes of the slice: x: 4 (x_hi: 2, x_lo: 2; x = x_hi * 2 + x_lo), y: 4, z: 8, core: 2. Of those that a mesh axis runs over, the one named last changes fastest.
Arguments:
- focusing: bfloat16 [12, 2, 4096, 4096], P('bin', None, 'row'), may hold values from -0.0625 to 0.0625
- snapshots: bfloat16 [12, 2, 4096, 128], P('bin', None, 'row'), may hold values from -6 to 6
Outputs:
- spectrum: float32 [2, 4096, 4096], P(None, 'row', 'bin')
All inputs are finite; a program needn't handle non-finite values.
Results may differ from a plain program's by a relative error of at most 0.0034.
Values may be sent and summed in bfloat16 or wider, within the bound.
A program may use at most 64 MiB of HBM per device.

v0:
```python
import jax
import jax.numpy as jnp
from jax import lax
from jax.sharding import PartitionSpec as P


def contract(left, right):
    return lax.dot_general(
        left, right, (((1,), (1,)), ((), ())), preferred_element_type=jnp.float32
    )


def on_device(focusing, snapshots):
    local_bins = focusing.shape[0]
    own_rows = focusing.shape[2]
    width = focusing.shape[3]
    count = snapshots.shape[3]
    scale = 1.0 / (local_bins * lax.axis_size("bin") * count)
    pieces = []
    for index in range(local_bins):
        matrix = focusing[index]
        piece = lax.all_gather(snapshots[index], "row", axis=1, tiled=True)
        new_real = jnp.dot(matrix[0], piece[0], preferred_element_type=jnp.float32) - jnp.dot(
            matrix[1], piece[1], preferred_element_type=jnp.float32
        )
        new_imag = jnp.dot(matrix[0], piece[1], preferred_element_type=jnp.float32) + jnp.dot(
            matrix[1], piece[0], preferred_element_type=jnp.float32
        )
        pieces.append(jnp.stack([new_real, new_imag]).astype(jnp.bfloat16))
    focused = jnp.stack(pieces)
    total = jnp.zeros((2, own_rows, width), jnp.float32)
    for index in range(local_bins):
        current = focused[index]
        gram_piece = lax.all_gather(current, "row", axis=1, tiled=True)
        real_part = contract(current[0], gram_piece[0]) + contract(current[1], gram_piece[1])
        imag_part = contract(current[1], gram_piece[0]) - contract(current[0], gram_piece[1])
        total = total + jnp.stack([real_part, imag_part])
    return lax.psum_scatter(total * scale, "bin", scatter_dimension=2, tiled=True)


def solution(mesh):
    placed = (P("bin", None, "row", None), P("bin", None, "row", None))
    return jax.shard_map(
        on_device, mesh=mesh, in_specs=placed, out_specs=P(None, "row", "bin"), check_vma=False
    )
```

profile of v0, /device:TPU:1, one launch (start us, length us, event | category | flops | bytes accessed | tf_op | source)
XLA Modules:
  0.0 767.7 jit_solution(13210433172321638339)
XLA Ops:
  6.5 1.6 fusion.50
  8.1 0.0 all-gather.20.cloned.1.call-start
  8.2 0.7 all-gather.20.cloned.1.call-update
  8.9 0.0 all-gather.16.cloned.1.call-start
  8.9 0.7 all-gather.16.cloned.1.call-update
  9.6 0.0 all-gather.12.cloned.1.call-start
  9.7 119.6 %all-gather.18.cloned.1.call-done = bf16[1,2,4096,128]{3,2,1,0:T(8,128)(2,1)} async-done(((bf16[1,2,64,128]{3,2,1,0:T(8,128)(2,1)}), bf16[1,2,4096,128]{3,2,1,0:T(8,128)(2,1)}) %all-gather.18.cloned.1.call-update) | async-done | bytes 2097168 | tf_op jit(solution)/shard_map/all_gather | solution.py:22
  129.2 1.7 fusion.18
  131.0 1.8 fusion.19
  132.8 1.5 fusion.10
  134.4 0.3 fusion.11
  134.7 0.6 pad_maximum_fusion.1
  135.3 0.0 all-gather.14.cloned.1.call-start
  135.4 112.2 %all-gather.20.cloned.1.call-done = bf16[1,2,4096,128]{3,2,1,0:T(8,128)(2,1)} async-done(((bf16[1,2,64,128]{3,2,1,0:T(8,128)(2,1)}), bf16[1,2,4096,128]{3,2,1,0:T(8,128)(2,1)}) %all-gather.20.cloned.1.call-update) | async-done | bytes 2097168 | tf_op jit(solution)/shard_map/all_gather | solution.py:22
  247.5 1.7 fusion.22
  249.2 1.5 fusion.23
  250.8 0.3 fusion.12
  251.1 0.3 fusion.13
  251.4 0.6 pad_maximum_fusion.2
  252.1 0.0 all-gather.10.cloned.1.call-start
  252.1 113.7 %all-gather.16.cloned.1.call-done = bf16[1,2,4096,128]{3,2,1,0:T(8,128)(2,1)} async-done(((bf16[1,2,64,128]{3,2,1,0:T(8,128)(2,1)}), bf16[1,2,4096,128]{3,2,1,0:T(8,128)(2,1)}) %all-gather.16.cloned.1.call-update) | async-done | bytes 2097168 | tf_op jit(solution)/shard_map/all_gather | solution.py:22
  365.9 1.7 fusion.14
  367.5 1.5 fusion.15
  369.1 0.3 fusion.8
  369.4 0.3 fusion.9
  369.7 0.6 pad_maximum_fusion
  370.4 0.0 reduce-scatter.2.cloned.1.call-start
  370.4 113.6 %all-gather.12.cloned.1.call-done = bf16[2,4096,128]{2,1,0:T(8,128)(2,1)} async-done(((bf16[2,64,128]{2,1,0:T(8,128)(2,1)}), bf16[2,4096,128]{2,1,0:T(8,128)(2,1)}) %all-gather.12.cloned.1.call-update) | async-done | bytes 2097168 | tf_op jit(solution)/shard_map/all_gather | solution.py:34
  484.0 2.8 fusion.21
  486.8 1.5 fusion.20
  488.3 113.9 %all-gather.14.cloned.1.call-done = bf16[2,4096,128]{2,1,0:T(8,128)(2,1)} async-done(((bf16[2,64,128]{2,1,0:T(8,128)(2,1)}), bf16[2,4096,128]{2,1,0:T(8,128)(2,1)}) %all-gather.14.cloned.1.call-update) | async-done | bytes 2097168 | tf_op jit(solution)/shard_map/all_gather | solution.py:34
  602.2 2.8 fusion.25
  605.0 0.5 fusion.24
  605.5 114.8 %all-gather.10.cloned.1.call-done = bf16[2,4096,128]{2,1,0:T(8,128)(2,1)} async-done(((bf16[2,64,128]{2,1,0:T(8,128)(2,1)}), bf16[2,4096,128]{2,1,0:T(8,128)(2,1)}) %all-gather.10.cloned.1.call-update) | async-done | bytes 2097168 | tf_op jit(solution)/shard_map/all_gather | solution.py:34
  720.3 1.8 fusion.17
  722.2 0.1 copy-done.3
  722.2 0.5 fusion.16
  722.7 0.5 fusion.2
  723.2 0.7 copy-done.4
  723.9 0.5 fusion.3
  724.4 1.1 copy-done.2
  725.5 0.3 copy-done.5
  725.8 0.5 fusion.4
  726.3 0.5 fusion.5
  726.8 0.5 fusion
  727.3 0.5 fusion.1
  727.7 1.7 fusion.7
  729.5 31.4 %reduce-scatter.2.cloned.1.call-done = f32[2,64,1024]{2,1,0:T(8,128)} async-done(((f32[2,64,4096]{2,1,0:T(8,128)}), f32[2,64,1024]{2,1,0:T(8,128)}) %reduce-scatter.2.cloned.1.call-update) | async-done | bytes 524304 | tf_op jit(solution)/shard_map/reduce_scatter | solution.py:38
  (24 shorter events, 0.1 us)
Async XLA Ops:
  6.5 126.3 %copy-start.7 = (bf16[3,2,64,4096]{3,2,1,0:T(8,128)(2,1)S(1)}, bf16[3,2,64,4096]{3,2,1,0:T(8,128)(2,1)}, u32[]{:S(2)}) copy-start(bf16[3,2,64,4096]{3,2,1,0:T(8,128)(2,1)} %param.2) | copy-start | bytes 9437188
  6.5 122.7 %all-gather.18.cloned.1.call-start = ((), (), s32[]{:S(2)}) async-start(), calls=%async_computation.6 | async-start | bytes 2129920 | tf_op jit(solution)/shard_map/all_gather | solution.py:22
  8.1 239.4 %all-gather.20.cloned.1.call-start = ((), (), s32[]{:S(2)}) async-start(), calls=%async_computation.7 | async-start | bytes 2129920 | tf_op jit(solution)/shard_map/all_gather | solution.py:22
  8.9 357.0 %all-gather.16.cloned.1.call-start = ((), (), s32[]{:S(2)}) async-start(), calls=%async_computation.5 | async-start | bytes 2129920 | tf_op jit(solution)/shard_map/all_gather | solution.py:22
  9.6 474.4 %all-gather.12.cloned.1.call-start = ((), (), s32[]{:S(2)}) async-start(), calls=%async_computation.2 | async-start | bytes 2129920 | tf_op jit(solution)/shard_map/all_gather | solution.py:34
  130.9 3.4 copy-start.10
  135.3 466.8 %all-gather.14.cloned.1.call-start = ((), (), s32[]{:S(2)}) async-start(), calls=%async_computation.3 | async-start | bytes 2129920 | tf_op jit(solution)/shard_map/all_gather | solution.py:34
  247.5 3.2 copy-start.9
  252.1 468.2 %all-gather.10.cloned.1.call-start = ((), (), s32[]{:S(2)}) async-start(), calls=%async_computation.1 | async-start | bytes 2129920 | tf_op jit(solution)/shard_map/all_gather | solution.py:34
  365.9 3.2 copy-start.8
  370.4 390.5 %reduce-scatter.2.cloned.1.call-start = ((), (), s32[]{:S(2)}) async-start(), calls=%async_computation.4 | async-start | bytes 2621440 | tf_op jit(solution)/shard_map/reduce_scatter | solution.py:38
  484.0 2.8 copy-start
  602.2 2.8 copy-start.1
  720.3 1.9 copy-start.3
  720.3 2.4 copy-start.6
  722.7 1.2 copy-start.4
  723.9 1.6 copy-start.2
  723.9 1.9 copy-start.5
Sparse Core Ops, SparseCore 0:
  10.9 118.3 all-gather.17
  132.7 114.7 all-gather.19
  251.1 114.7 all-gather.15
  369.2 114.7 all-gather.11
  487.4 114.7 all-gather.13
  605.5 114.7 all-gather.9
  729.6 31.2 reduce-scatter.1
where the time goes:
time: 768 us
  waiting for transfers between devices  721 us (94%)
  matrix products  25.9 us (3%)
  between operations  13.7 us (2%)
    all_gather x3, waiting for transfers between devices, on_device(): piece = lax.all_gather(snapshots[index], 'row', axis=1, tiled=True)  345 us
    all_gather x3, waiting for transfers between devices, on_device(): gram_piece = lax.all_gather(current, 'row', axis=1, tiled=True)  342 us
    reduce_scatter x1, waiting for transfers between devices, on_device(): lax.psum_scatter(total * scale, 'bin', scatter_dimension=2, tiled=True)  31.4 us
  transfers between devices with their start and end apart: 7, of which 7 were waited for; matrix products, arithmetic and copies ran while one was open for 3% of the time, Pallas kernels for 0%

commit v1 on v0

--- a/solution.py
+++ b/solution.py
@@ -31,7 +31,9 @@
     total = jnp.zeros((2, own_rows, width), jnp.float32)
     for index in range(local_bins):
         current = focused[index]
-        gram_piece = lax.all_gather(current, "row", axis=1, tiled=True)
+        gram_piece = jnp.concatenate(
+            lax.all_to_all(jnp.stack([current] * lax.axis_size("row")), "row", 0, 0), axis=1
+        )
         real_part = contract(current[0], gram_piece[0]) + contract(current[1], gram_piece[1])
         imag_part = contract(current[1], gram_piece[0]) - contract(current[0], gram_piece[1])
         total = total + jnp.stack([real_part, imag_part])

time: 768 us -> 486 us (0.63)
  waiting for transfers between devices: 721 us -> 405 us
  starting transfers between devices: 0.25 us -> 23.7 us
  local copies, waits for them, and re-layouts: 3.76 us -> 12.3 us
    all_gather x3 -> x0, waiting for transfers between devices: 342 us -> none  [on_device(): gram_piece = lax.all_gather(current, 'row', axis=1, tiled=True)]
    all_to_all x0 -> x3, waiting for transfers between devices: none -> 36.8 us  [on_device(): lax.all_to_all(jnp.stack([current] * lax.axis_size('row')), 'row', 0, 0)]
    all_to_all x0 -> x3, starting transfers between devices: none -> 23.6 us  [on_device(): lax.all_to_all(jnp.stack([current] * lax.axis_size('row')), 'row', 0, 0)]
    all_gather x3, waiting for transfers between devices: 345 us -> 332 us  [on_device(): piece = lax.all_gather(snapshots[index], 'row', axis=1, tiled=True)]
  transfers between devices with their start and end apart: 7 -> 7, of which waited for: 7 -> 5; matrix products, arithmetic and copies ran while one was open for 3% -> 6% of each run, Pallas kernels for 0% -> 0%
where the time goes in v1:
time: 486 us; the launch traced here: 485 us
  waiting for transfers between devices  405 us (83%)
  matrix products  28.5 us (6%)
  starting transfers between devices  23.7 us (5%)
  between operations  13.4 us (3%)
  local copies, waits for them, and re-layouts  12.3 us (3%)
    all_gather x3, waiting for transfers between devices, on_device(): piece = lax.all_gather(snapshots[index], 'row', axis=1, tiled=True)  332 us
    all_to_all x3, waiting for transfers between devices, on_device(): lax.all_to_all(jnp.stack([current] * lax.axis_size('row')), 'row', 0, 0)  36.8 us
    reduce_scatter x1, waiting for transfers between devices, on_device(): lax.psum_scatter(total * scale, 'bin', scatter_dimension=2, tiled=True)  34.6 us
    all_to_all x3, starting transfers between devices, on_device(): lax.all_to_all(jnp.stack([current] * lax.axis_size('row')), 'row', 0, 0)  23.6 us
    dot_general x12, matrix products, contract(): lax.dot_general(left, right, (((1,), (1,)), ((), ())), preferred_element_...  9.78 us
  transfers between devices with their start and end apart: 7, of which 5 were waited for; matrix products, arithmetic and copies ran while one was open for 6% of the time, Pallas kernels for 0%

profile of v1, /device:TPU:1, one launch (start us, length us, event | category | flops | bytes accessed | tf_op | source)
XLA Modules:
  0.0 484.9 jit_solution(7769427793199661296)
XLA Ops:
  6.5 1.4 fusion.47
  8.0 0.0 all-gather.7.cloned.1.call-start
  8.0 0.7 all-gather.7.cloned.1.call-update
  8.7 120.5 %all-gather.11.cloned.1.call-done = bf16[1,2,4096,128]{3,2,1,0:T(8,128)(2,1)} async-done(((bf16[1,2,64,128]{3,2,1,0:T(8,128)(2,1)}), bf16[1,2,4096,128]{3,2,1,0:T(8,128)(2,1)}) %all-gather.11.cloned.1.call-update) | async-done | bytes 2097168 | tf_op jit(solution)/shard_map/all_gather | solution.py:22
  129.2 1.8 fusion.19
  131.1 1.7 fusion.18
  132.8 1.4 fusion.13
  134.2 1.4 fusion.12
  135.5 1.9 stack.92
  137.4 7.7 %all-to-all-start.2 = ((bf16[64,2,64,128]{3,2,1,0:T(8,128)(2,1)}), bf16[64,2,64,128]{3,2,1,0:T(8,128)(2,1)S(1)}, u32[]{:S(2)}, u32[]{:S(2)}) async-start(bf16[64,2,64,128]{3,2,1,0:T(8,128)(2,1)} %stack.92), calls=%async_computation.2 | async-start | bytes 4194304 | tf_op jit(solution)/shard_map/all_to_all | solution.py:35
  145.2 0.7 all-gather.9.cloned.1.call-update
  145.9 105.5 %all-gather.7.cloned.1.call-done = bf16[1,2,4096,128]{3,2,1,0:T(8,128)(2,1)} async-done(((bf16[1,2,64,128]{3,2,1,0:T(8,128)(2,1)}), bf16[1,2,4096,128]{3,2,1,0:T(8,128)(2,1)}) %all-gather.7.cloned.1.call-update) | async-done | bytes 2097168 | tf_op jit(solution)/shard_map/all_gather | solution.py:22
  251.4 1.8 fusion.15
  253.2 1.7 fusion.14
  254.9 1.4 fusion.9
  256.3 1.4 fusion.8
  257.7 1.9 stack.78
  259.6 7.9 %all-to-all-start = ((bf16[64,2,64,128]{3,2,1,0:T(8,128)(2,1)}), bf16[64,2,64,128]{3,2,1,0:T(8,128)(2,1)}, u32[]{:S(2)}, u32[]{:S(2)}) async-start(bf16[64,2,64,128]{3,2,1,0:T(8,128)(2,1)} %stack.78), calls=%async_computation | async-start | bytes 4194304 | tf_op jit(solution)/shard_map/all_to_all | solution.py:35
  267.5 106.5 %all-gather.9.cloned.1.call-done = bf16[1,2,4096,128]{3,2,1,0:T(8,128)(2,1)} async-done(((bf16[1,2,64,128]{3,2,1,0:T(8,128)(2,1)}), bf16[1,2,4096,128]{3,2,1,0:T(8,128)(2,1)}) %all-gather.9.cloned.1.call-update) | async-done | bytes 2097168 | tf_op jit(solution)/shard_map/all_gather | solution.py:22
  374.0 1.8 fusion.17
  375.8 1.7 fusion.16
  377.6 1.4 fusion.11
  378.9 1.4 fusion.10
  380.3 1.9 stack.85
  382.2 7.9 %all-to-all-start.1 = ((bf16[64,2,64,128]{3,2,1,0:T(8,128)(2,1)}), bf16[64,2,64,128]{3,2,1,0:T(8,128)(2,1)}, u32[]{:S(2)}, u32[]{:S(2)}) async-start(bf16[64,2,64,128]{3,2,1,0:T(8,128)(2,1)} %stack.85), calls=%async_computation.1 | async-start | bytes 4194304 | tf_op jit(solution)/shard_map/all_to_all | solution.py:35
  390.1 0.0 reduce-scatter.2.cloned.1.call-start
  390.2 0.2 fusion.44
  390.4 1.4 fusion.53
  391.8 1.6 fusion.52
  393.4 1.7 fusion.46
  395.1 1.5 fusion.49
  396.6 1.4 fusion.48
  398.0 36.8 %all-to-all-done.1 = bf16[64,2,64,128]{3,2,1,0:T(8,128)(2,1)} async-done(((bf16[64,2,64,128]{3,2,1,0:T(8,128)(2,1)}), bf16[64,2,64,128]{3,2,1,0:T(8,128)(2,1)}, u32[]{:S(2)}, u32[]{:S(2)}) %all-to-all-start.1) | async-done | bytes 2097184 | tf_op jit(solution)/shard_map/all_to_all | solution.py:35
  434.9 1.7 fusion.45
  436.6 0.5 fusion.51
  437.1 0.5 fusion.50
  437.6 0.2 copy-done.3
  437.8 0.5 fusion.5
  438.3 0.6 copy-done.1
  438.9 0.5 fusion.4
  439.4 0.7 copy-done.2
  440.1 0.5 fusion.1
  440.6 0.1 copy-done
  440.7 0.5 fusion
  441.2 0.5 fusion.3
  441.6 0.5 fusion.2
  442.1 1.7 fusion.7
  443.8 34.6 %reduce-scatter.2.cloned.1.call-done = f32[2,64,1024]{2,1,0:T(8,128)} async-done(((f32[2,64,4096]{2,1,0:T(8,128)}), f32[2,64,1024]{2,1,0:T(8,128)}) %reduce-scatter.2.cloned.1.call-update) | async-done | bytes 524304 | tf_op jit(solution)/shard_map/reduce_scatter | solution.py:40
  (19 shorter events, 0.1 us)
Async XLA Ops:
  6.5 122.7 %all-gather.11.cloned.1.call-start = ((), (), s32[]{:S(2)}) async-start(), calls=%async_computation.7 | async-start | bytes 2129920 | tf_op jit(solution)/shard_map/all_gather | solution.py:22
  8.0 243.4 %all-gather.7.cloned.1.call-start = ((), (), s32[]{:S(2)}) async-start(), calls=%async_computation.5 | async-start | bytes 2129920 | tf_op jit(solution)/shard_map/all_gather | solution.py:22
  129.2 3.6 copy-start.6
  137.4 120.2 %all-to-all-start.2 = ((bf16[64,2,64,128]{3,2,1,0:T(8,128)(2,1)}), bf16[64,2,64,128]{3,2,1,0:T(8,128)(2,1)S(1)}, u32[]{:S(2)}, u32[]{:S(2)}) async-start(bf16[64,2,64,128]{3,2,1,0:T(8,128)(2,1)} %stack.92), calls=%async_computation.2 | async-start | bytes 4194304 | tf_op jit(solution)/shard_map/all_to_all | solution.py:35
  145.1 228.9 %all-gather.9.cloned.1.call-start = ((), (), s32[]{:S(2)}) async-start(), calls=%async_computation.6 | async-start | bytes 2129920 | tf_op jit(solution)/shard_map/all_gather | solution.py:22
  251.4 3.6 copy-start.4
  259.6 120.7 %all-to-all-start = ((bf16[64,2,64,128]{3,2,1,0:T(8,128)(2,1)}), bf16[64,2,64,128]{3,2,1,0:T(8,128)(2,1)}, u32[]{:S(2)}, u32[]{:S(2)}) async-start(bf16[64,2,64,128]{3,2,1,0:T(8,128)(2,1)} %stack.78), calls=%async_computation | async-start | bytes 4194304 | tf_op jit(solution)/shard_map/all_to_all | solution.py:35
  374.0 3.6 copy-start.5
  382.2 52.7 %all-to-all-start.1 = ((bf16[64,2,64,128]{3,2,1,0:T(8,128)(2,1)}), bf16[64,2,64,128]{3,2,1,0:T(8,128)(2,1)}, u32[]{:S(2)}, u32[]{:S(2)}) async-start(bf16[64,2,64,128]{3,2,1,0:T(8,128)(2,1)} %stack.85), calls=%async_computation.1 | async-start | bytes 4194304 | tf_op jit(solution)/shard_map/all_to_all | solution.py:35
  390.1 88.2 %reduce-scatter.2.cloned.1.call-start = ((), (), s32[]{:S(2)}) async-start(), calls=%async_computation.4 | async-start | bytes 2621440 | tf_op jit(solution)/shard_map/reduce_scatter | solution.py:40
  436.6 1.2 copy-start.3
  437.6 1.3 copy-start.1
  438.9 1.2 copy-start.2
  439.4 1.3 copy-start
Sparse Core Ops, SparseCore 0:
  10.9 118.3 all-gather.10
  132.7 118.5 all-gather.6
  254.9 119.0 all-gather.8
  443.9 34.4 reduce-scatter.1
